TPU v7x, 32 devices: a whole 2x2x4 slice. The times are simulated.
32 devices in a mesh: groups: 2 (over y), pb: 4 (over z), pt: 2 (over x), spin: 2 (over core).
Axes of the slice: x: 2, y: 2, z: 4, core: 2. Of those that a mesh axis runs over, the one named last changes fastest.
Arguments:
- amplitudes: float32 [4, 4, 2048], P(('groups', 'spin'), 'pb'), parts along dimension 0, may hold values from -6 to 6
- valence_orbitals: float32 [4, 4, 32, 1024], P(('groups', 'spin'), 'pb', None, 'pt'), parts along dimension 0, may hold values from -1 to 1
- conduction_orbitals: float32 [4, 4, 64, 1024], P(('groups', 'spin'), 'pb', None, 'pt'), parts along dimension 0, may hold values from -0.75 to 0.75
- screened: float32 [8, 1024, 1024], P(('groups', 'pb'), 'pt'), parts along dimension 0, may hold values from -0.125 to 0.125
- band_gaps: float32 [4, 4, 2048], P(('groups', 'spin'), 'pb', 'pt'), parts along dimension 0, may hold values from 0.5 to 2
- shifts: float32 [4], P(('groups', 'spin')), parts along dimension 0, may hold values from 0.2 to 1
- difference_table: int32 [4, 4], replicated, may hold values from 0 to 3, as said below
Outputs:
- corrections: float32 [4, 4, 2048], P(('groups', 'spin'), 'pb', 'pt'), parts along dimension 0
There are 2 independent parts, one for each index of `groups`. A program takes and returns all parts, laid end to end along the dimension named above; an argument that names none is the same for every part. Nothing has to cross between parts.
Inputs may be any that keep to these rules, and one draw needn't show every extreme that they name: Every column of difference_table is a permutation of the 4 k-points: entry [k, q] is the k-point k - q on the k-point grid.
All inputs are finite; a program needn't handle non-finite values.
Results may differ from a plain program's by a relative error of at most 0.0003.
Values sent between devices are 32-bit elements; how exact they have to be, the bound alone decides.
A program may use at most 64 MiB of HBM per device.

v0:
```python
import jax
import jax.numpy as jnp
from jax import lax
from jax.sharding import PartitionSpec as P


def pair_block(inputs, amp_all, valence_all, fetch_rows, weight):
    target_ids, source_ids = inputs
    nbands = valence_all.shape[1]
    source_amp = jnp.take(amp_all, source_ids, axis=0)
    source_amp = source_amp.reshape(source_amp.shape[0], nbands, -1)
    source_val = jnp.take(valence_all, source_ids, axis=0)
    target_val = jnp.take(valence_all, target_ids, axis=0)
    source_con = fetch_rows(source_ids)
    target_con = fetch_rows(target_ids)
    slabs = source_con.shape[1]
    shaped_weight = weight.reshape(weight.shape[0], slabs, -1)
    mixed = jnp.einsum("bvm,bvc->bcm", source_val, source_amp, precision=lax.Precision.HIGHEST)
    pairs = jnp.einsum("bcm,bpcs->bmps", mixed, source_con, precision=lax.Precision.HIGHEST)
    pairs = pairs * shaped_weight[None]
    half = jnp.einsum("bvm,bmps->bvps", target_val, pairs, precision=lax.Precision.HIGHEST)
    result = jnp.einsum("bvps,bpcs->bvc", half, target_con, precision=lax.Precision.HIGHEST)
    return result.reshape(result.shape[0], -1)


def shards(
    amplitudes, valence_orbitals, conduction_orbitals, screened, band_gaps, shifts, difference_table
):
    conduction_points = lax.all_gather(conduction_orbitals, "pt", axis=3, tiled=True)
    amp_all, valence_all, conduction_all = (
        lax.all_gather(amplitudes, "pb", axis=1, tiled=True),
        lax.all_gather(valence_orbitals, "pb", axis=1, tiled=True),
        lax.all_gather(conduction_points, "pb", axis=1, tiled=True),
    )
    conduction_rows = conduction_all[0]

    def fetch_rows(ids):
        return jnp.take(conduction_rows, ids, axis=0)[:, None]

    amp_all = amp_all[0]
    valence_all = valence_all[0]
    total_k = amp_all.shape[0]
    blocks = total_k // 4
    target_ids = jnp.arange(total_k, dtype=jnp.int32).reshape(blocks, 4)
    local_count = screened.shape[0]
    transfer = lax.axis_index("pb") * local_count + 0
    sources = lax.dynamic_index_in_dim(difference_table, transfer, 1, keepdims=False)
    weight = screened[0]

    def run_block(inputs):
        return pair_block(inputs, amp_all, valence_all, fetch_rows, weight)

    blocked = lax.map(run_block, (target_ids, sources.reshape(blocks, 4)))
    direct = blocked.reshape(total_k, -1)
    terms = direct[None]
    partial_sum = lax.psum_scatter(terms, "pb", scatter_dimension=1, tiled=True)
    summed = lax.psum_scatter(partial_sum, "pt", scatter_dimension=2, tiled=True)
    column_width = band_gaps.shape[2]
    own_amp = lax.dynamic_slice_in_dim(
        amplitudes, lax.axis_index("pt") * column_width, column_width, 2
    )
    return (band_gaps * own_amp - summed) / (band_gaps + shifts[:, None, None])


def solution(mesh):
    placed = (
        P(("groups", "spin"), "pb", None),
        P(("groups", "spin"), "pb", None, "pt"),
        P(("groups", "spin"), "pb", None, "pt"),
        P(("groups", "pb"), "pt", None),
        P(("groups", "spin"), "pb", "pt"),
        P(("groups", "spin")),
        P(),
    )
    return jax.shard_map(
        shards,
        mesh=mesh,
        in_specs=placed,
        out_specs=P(("groups", "spin"), "pb", "pt"),
        check_vma=False,
    )
```

profile of v0, /device:TPU:0, one launch (start us, length us, event | category | flops | bytes accessed | tf_op | source)
XLA Modules:
  0.0 115.9 jit_solution(12010350565428244047)
XLA Ops:
  6.5 0.0 all-gather.2.cloned.1.call-start
  6.5 8.9 %all_gather.14 = f32[1,1,64,1024]{3,2,0,1:T(8,128)} all-gather(f32[1,1,64,512]{3,2,0,1:T(8,128)} %bitcast.30), channel_id=1, replica_groups=mesh['groups'=2,'pb'=4,'pt'=2,'spin'=2] {'pt'}, dimensions={3}, use_global_device_ids=true | all-gather | bytes 393216 | tf_op jit(solution)/shard_map/all_gather | solution.py:29
  15.5 0.0 all-gather.2.cloned.1.call-update
  15.5 0.0 reduce-scatter.5.cloned.1.call-start
  15.6 13.6 %all_gather.13 = f32[1,4,2048]{2,0,1:T(1,128)S(1)} all-gather(f32[1,1,2048]{2,0,1:T(1,128)} %bitcast.32), channel_id=1, replica_groups=mesh['groups'=2,'pb'=4,'pt'=2,'spin'=2] {'pb'}, dimensions={1}, use_global_device_ids=true | all-gather | bytes 40960 | tf_op jit(solution)/shard_map/all_gather | solution.py:31
  29.2 0.9 fusion.21
  30.1 0.6 gather_fusion
  30.7 0.1 gather.14
  30.8 16.3 %all_gather.12 = f32[1,4,32,512]{3,2,0,1:T(8,128)S(1)} all-gather(f32[1,1,32,512]{3,2,0,1:T(8,128)} %bitcast.31), channel_id=1, replica_groups=mesh['groups'=2,'pb'=4,'pt'=2,'spin'=2] {'pb'}, dimensions={1}, use_global_device_ids=true | all-gather | bytes 327680 | tf_op jit(solution)/shard_map/all_gather | solution.py:32
  47.2 0.6 gather_fusion.2
  47.8 0.6 gather_fusion.1
  48.3 1.2 %dynamic-slice = u32[1]{0:T(128)} dynamic-slice(u32[32]{0:T(128)} %constant.80, u32[]{:T(128)S(6)} %add.49), dynamic_slice_sizes={1} | dynamic-slice | bytes 12
  49.6 0.9 and_reduce_fusion
  50.5 0.7 fusion.11
  51.2 0.0 all-gather.2.cloned.1.call-done
  51.2 1.8 %gather_fusion.3 = f32[4,64,1024]{2,1,0:T(8,128)S(1)} fusion(f32[4,64,1024]{2,1,0:T(8,128)} %bitcast.22, s32[1024]{0:T(1024)S(1)} %pad_clamp_fusion), kind=kCustom, calls=%fused_computation.1.clone | custom fusion | bytes 2097168 | tf_op jit(solution)/shard_map/while/body/eval_jaxpr/jit(_take)/gather | solution.py:38
  53.1 1.8 %gather_fusion.4 = f32[4,64,1024]{2,1,0:T(8,128)S(1)} fusion(f32[4,64,1024]{2,1,0:T(8,128)} %bitcast.23, s32[1024]{0:T(1024)S(1)} %pad_clamp_fusion.2), kind=kCustom, calls=%fused_computation.3.clone | custom fusion | bytes 2097168 | tf_op jit(solution)/shard_map/while/body/eval_jaxpr/jit(_take)/gather | solution.py:38
  54.9 0.0 copy-start
  54.9 6.9 %fusion.5 = f32[4,512,1024]{2,1,0:T(8,128)S(1)} fusion(f32[4,64,512]{2,1,0:T(8,128)S(1)} %fusion.11, f32[4,64,1024]{2,1,0:T(8,128)S(1)} %gather_fusion.3, pred[4]{0:T(512)(128)(4,1)S(1)} %compare_and_fusion), kind=kOutput, calls=%fused_computation.10 | convolution fusion | flops 1610874880 | bytes 9961476 | tf_op jit(solution)/shard_map/while/body/eval_jaxpr/bcm,bpcs->bmps/dot_general | solution.py:19
  61.8 0.0 copy-start.1
  61.8 0.0 copy-start.2
  61.9 5.1 %fusion = f32[4,32,1024]{2,1,0:T(8,128)S(1)} fusion(f32[4,512,1024]{2,1,0:T(8,128)S(1)} %fusion.5, f32[512,1024]{1,0:T(8,128)S(1)} %bitcast.28, f32[4,32,512]{2,1,0:T(8,128)S(1)} %gather_fusion.1, pred[4]{0:T(512)(128)(4,1)S(1)} %broadcast_compare_fusion), kind=kOutput, calls=%fused_computation.5 | convolution fusion | flops 807469056 | bytes 11272196 | tf_op jit(solution)/shard_map/while/body/eval_jaxpr/bvm,bmps->bvps/dot_general | solution.py:21
  67.0 1.1 fusion.3
  68.1 0.1 broadcast_in_dim.47
  68.1 18.5 %all-reduce = f32[1,4,2048]{2,1,0:T(4,128)S(1)} all-reduce(f32[1,4,2048]{2,1,0:T(4,128)S(1)} %broadcast_in_dim.47), channel_id=2, replica_groups=mesh['groups'=2,'pb'=4,'pt'=2,'spin'=2] {'pb'}, use_global_device_ids=true, to_apply=%region_0.3.clone | all-reduce | flops 8192 | bytes 65536
  86.7 0.7 constant_dynamic-slice_fusion
  87.4 1.9 %copy.13 = f32[1,1,2048]{1,0,2:T(1,128)} copy(f32[1,1,2048]{2,1,0:T(1,128)S(1)} %constant_dynamic-slice_fusion) | data formatting | bytes 16384
  89.3 0.0 reduce-scatter.5.cloned.1.call-update
  89.9 17.3 %reduce-scatter.5.cloned.1.call-done = f32[1024,1]{1,0:T(8,128)} async-done(((f32[2048,1]{1,0:T(8,128)}), f32[1024,1]{1,0:T(8,128)}) %reduce-scatter.5.cloned.1.call-update) | async-done | bytes 4112
  107.3 1.2 %copy.14 = f32[1,1,1024]{2,1,0:T(1,128)S(1)} copy(f32[1,1,1024]{1,0,2:T(1,128)} %bitcast.29) | data formatting | bytes 8192
  108.4 0.0 copy-done.2
  108.5 0.6 add_divide_fusion
  (10 shorter events, 0.1 us)
Async XLA Ops:
  6.5 44.7 %all-gather.2.cloned.1.call-start = ((), (), s32[]{:S(2)}) async-start(), calls=%async_computation.1 | async-start | bytes 1310720 | tf_op jit(solution)/shard_map/all_gather | solution.py:33
  15.5 91.8 %reduce-scatter.5.cloned.1.call-start = ((), (), s32[]{:S(2)}) async-start(), calls=%async_computation.2 | async-start | bytes 1572864
  54.9 6.9 %copy-start = (f32[1,512,1024]{2,1,0:T(8,128)S(1)}, f32[1,512,1024]{2,1,0:T(8,128)}, u32[]{:S(2)}) copy-start(f32[1,512,1024]{2,1,0:T(8,128)} %param.14) | copy-start | bytes 6291460
  61.8 46.6 %copy-start.1 = (f32[1,1,2048]{2,1,0:T(1,128)S(1)}, f32[1,1,2048]{2,1,0:T(1,128)}, u32[]{:S(2)}) copy-start(f32[1,1,2048]{2,1,0:T(1,128)} %param.11) | copy-start | bytes 24580
  61.8 46.6 %copy-start.2 = (f32[1,1,1024]{2,1,0:T(1,128)S(1)}, f32[1,1,1024]{2,1,0:T(1,128)}, u32[]{:S(2)}) copy-start(f32[1,1,1024]{2,1,0:T(1,128)} %param.15) | copy-start | bytes 12292
Sparse Core Ops, SparseCore 0:
  15.6 32.5 all-gather.1
  89.4 17.8 reduce-scatter.4
where the time goes:
time: 116 us
  blocking collectives  57.5 us (50%)
  waiting for transfers between devices  17.4 us (15%)
  between operations  14.2 us (12%)
  matrix products  13.8 us (12%)
  local copies, waits for them, and re-layouts  10.6 us (9%)
  other arithmetic  2.42 us (2%)
    unnamed x1, blocking collectives  18.5 us
    unnamed x3, waiting for transfers between devices  17.4 us
    all_gather x1, blocking collectives, shards(): lax.all_gather(valence_orbitals, 'pb', axis=1, tiled=True)  16.3 us
    all_gather x1, blocking collectives, shards(): lax.all_gather(amplitudes, 'pb', axis=1, tiled=True)  13.6 us
    all_gather x1, blocking collectives, shards(): lax.all_gather(conduction_orbitals, 'pt', axis=3, tiled=True)  8.95 us
    dot_general x1, matrix products, pair_block(): jnp.einsum('bcm,bpcs->bmps', mixed, source_con, precision=lax.Precision.H...  6.89 us
    dot_general x1, matrix products, pair_block(): jnp.einsum('bvm,bmps->bvps', target_val, pairs, precision=lax.Precision.H...  5.12 us
    unnamed x11, local copies, waits for them, and re-layouts  5 us
  transfers between devices with their start and end apart: 2, of which 1 were waited for; matrix products, arithmetic and copies ran while one was open for 5% of the time, Pallas kernels for 0%

commit v1 on v0

v1 whole, which is shorter than its diff:
```python
import functools

import jax
import jax.numpy as jnp
from jax import lax
from jax.experimental import pallas as pl
from jax.experimental.pallas import tpu as pltpu
from jax.sharding import PartitionSpec as P

F32 = jnp.float32
BF16 = jnp.bfloat16
LANES = 128


def split(x):
    hi = x.astype(BF16)
    return hi, (x - hi.astype(F32)).astype(BF16)


def dot(a, b, dims=((1,), (0,))):
    return lax.dot_general(a, b, (dims, ((), ())), preferred_element_type=F32)


def each(count, body):
    if count <= 4:
        for i in range(count):
            body(i)
    else:
        lax.fori_loop(0, count, lambda i, _: (body(i), 0)[1], 0)


def kernel(
    n, m, ch,
    amp_ref, val_ref, con_ref, scr_ref, gap_ref, shift_ref, table_ref,
    out_ref,
    amp_all, val_all, con_all, weight, gaps,
    amp_wide, val_stack, con_stack, mix, half_stack, part, inbox, total,
    load_sem, amp_send, amp_recv, val_send, val_recv, con_recv,
    conz_send, conx_send, part_send, part_recv,
):
    nv, slab = val_ref.shape
    nc = con_ref.shape[0]
    w = slab // ch
    q = lax.axis_index("pb")
    p = lax.axis_index("pt")

    def at(z, x):
        return {"pb": z, "pt": x}

    def remote(src, dst, send, recv, z, x):
        return pltpu.make_async_remote_copy(
            src_ref=src, dst_ref=dst, send_sem=send, recv_sem=recv,
            device_id=at(z, x), device_id_type=pl.DeviceIdType.MESH,
        )

    barrier = pltpu.get_barrier_semaphore()
    for dz in range(n):
        for dx in range(m):
            if dz or dx:
                pl.semaphore_signal(
                    barrier, inc=1, device_id=at(lax.rem(q + dz, n), lax.rem(p + dx, m)),
                    device_id_type=pl.DeviceIdType.MESH,
                )

    loads = [
        pltpu.make_async_copy(amp_ref, amp_all.at[q], load_sem.at[0]),
        pltpu.make_async_copy(val_ref, val_all.at[q], load_sem.at[1]),
        pltpu.make_async_copy(gap_ref, gaps, load_sem.at[2]),
        pltpu.make_async_copy(scr_ref, weight, load_sem.at[3]),
    ] + [
        pltpu.make_async_copy(
            con_ref.at[:, pl.ds(c * w, w)], con_all.at[q, p, c], load_sem.at[4 + c]
        )
        for c in range(ch)
    ]
    for load in loads:
        load.start()

    pl.semaphore_wait(barrier, n * m - 1)

    def val_copy(z):
        return remote(val_ref, val_all.at[q], val_send.at[z], val_recv.at[q], z, p)

    def amp_copy(z):
        return remote(amp_ref, amp_all.at[q], amp_send.at[z], amp_recv.at[q], z, p)

    def send_small(d):
        z = lax.rem(q + d + 1, n)
        amp_copy(z).start()
        val_copy(z).start()

    each(n - 1, send_small)

    def con_z(s, c, side, src):
        z = q - 1 if side == 0 else q + 1
        return remote(
            src, con_all.at[s, p, c], conz_send.at[s, c, side], con_recv.at[s, p, c], z, p
        )

    def con_x(s, c, dx, src):
        x = lax.rem(p + dx, m)
        return remote(
            src, con_all.at[s, p, c], conx_send.at[s, dx - 1, c], con_recv.at[s, p, c], q, x
        )

    def con_wait(s, x, c):
        block = con_all.at[s, x, c]
        pltpu.make_async_remote_copy(
            src_ref=block, dst_ref=block, send_sem=conz_send.at[s, c, 0],
            recv_sem=con_recv.at[s, x, c], device_id=at(q, lax.rem(p + 1, m)),
            device_id_type=pl.DeviceIdType.MESH,
        ).wait_recv()

    for c in range(ch):
        own = con_ref.at[:, pl.ds(c * w, w)]

        @pl.when(q > 0)
        def _():
            con_z(q, c, 0, own).start()

        @pl.when(q < n - 1)
        def _():
            con_z(q, c, 1, own).start()

        for dx in range(1, m):
            con_x(q, c, dx, own).start()

    def prepare(s):
        rows = amp_all[s]
        turned = pltpu.roll(rows, LANES // 2, 1)
        low = lax.broadcasted_iota(jnp.int32, rows.shape, 1) < LANES // 2
        amp_wide[pl.ds(0, nv // 2, stride=2), :] = jnp.where(low, rows, turned)
        amp_wide[pl.ds(1, nv // 2, stride=2), :] = jnp.where(low, turned, rows)
        a_hi, a_lo = split(amp_wide[pl.ds(0, nv), :])
        v_hi, v_lo = split(val_all[s])
        both = jnp.concatenate([v_hi, v_lo], axis=0)
        val_stack[s] = both
        mixed = dot(
            jnp.concatenate([both, both], axis=0),
            jnp.concatenate([a_hi, a_hi, a_lo, a_lo], axis=0),
            ((0,), (0,)),
        )
        hi = mixed.astype(BF16).astype(F32)
        left = lax.broadcasted_iota(jnp.int32, mixed.shape, 1) < LANES // 2
        pair = jnp.where(left, hi, mixed - hi).astype(BF16)
        mix[s] = jnp.concatenate([pair, pair], axis=1)

    def target_of(s):
        if n <= 8:
            found = jnp.int32(0)
            for k in range(1, n):
                found = jnp.where(table_ref[k, q] == s, k, found)
            return found
        return lax.fori_loop(
            0, n, lambda k, f: jnp.where(table_ref[k, q] == s, k, f), jnp.int32(0)
        )

    def unit(s, x, c, target):
        c_hi, c_lo = split(con_all[s, x, c])
        stack = jnp.concatenate([c_hi, c_hi, c_lo, c_lo], axis=0)
        con_stack[s, x, c] = stack
        columns = pl.ds(pl.multiple_of(x * slab + c * w, w), w)
        pairs = dot(mix[s], stack) * weight[:, columns]
        p_hi, p_lo = split(pairs)
        bands = val_stack[target]
        both = dot(bands, p_hi) + dot(bands, p_lo)
        half = both[:nv] + both[nv:]
        h_hi, h_lo = split(half)
        half_stack[s, x, c] = jnp.concatenate([h_hi, h_lo], axis=0)

    def units(s, x):
        target = target_of(s)
        lax.fori_loop(0, ch, lambda c, _: (unit(s, x, c, target), 0)[1], 0)

    def crossed(s):
        target = target_of(s)

        def step(i, _):
            x = lax.rem(p + 1 + lax.div(i, ch), m)
            c = lax.rem(i, ch)
            con_wait(s, x, c)
            unit(s, x, c, target)
            return 0

        lax.fori_loop(0, (m - 1) * ch, step, 0)

    for load in loads:
        load.wait()
    prepare(q)

    def take_small(d):
        s = lax.rem(q + d + 1, n)
        remote(amp_all.at[s], amp_all.at[s], amp_send.at[s], amp_recv.at[s], s, p).wait_recv()
        remote(val_all.at[s], val_all.at[s], val_send.at[s], val_recv.at[s], s, p).wait_recv()
        prepare(s)

    lax.fori_loop(0, n - 1, lambda d, _: (take_small(d), 0)[1], 0)

    units(q, p)

    def forward(s, side):
        for c in range(ch):
            con_wait(s, p, c)
            block = con_all.at[s, p, c]

            @pl.when((q > 0) if side == 0 else (q < n - 1))
            def _():
                con_z(s, c, side, block).start()

            for dx in range(1, m):
                con_x(s, c, dx, block).start()

    def walk(t, _):
        @pl.when(q + t < n)
        def _():
            forward(q + t, 0)

        @pl.when(q - t >= 0)
        def _():
            forward(q - t, 1)

        @pl.when(q + t < n)
        def _():
            units(q + t, p)

        @pl.when(q - t >= 0)
        def _():
            units(q - t, p)

        @pl.when(q + t - 1 < n)
        def _():
            crossed(q + t - 1)

        @pl.when((q - t + 1 >= 0) & (t > 1))
        def _():
            crossed(q - t + 1)

        return 0

    lax.fori_loop(1, n, walk, 0)

    @pl.when(q + n - 1 < n)
    def _():
        crossed(q + n - 1)

    @pl.when((q - n + 1 >= 0) & (n > 1))
    def _():
        crossed(q - n + 1)

    def part_copy(k, x):
        return remote(
            part.at[k, x], inbox.at[q, p], part_send.at[k, x], part_recv.at[q, p], k, x
        )

    rows = nv // m

    def finish(d):
        k = lax.rem(q + d + 1, n)
        source = table_ref[k, q]
        acc = jnp.zeros((2 * nv, 2 * nc), F32)
        for x in range(m):
            for c in range(ch):
                acc = acc + dot(
                    half_stack[source, x, c], con_stack[k, x, c, nc : 3 * nc], ((1,), (1,))
                )
        acc = acc[:nv] + acc[nv:]
        direct = acc[:, :nc] + acc[:, nc:]
        for x in range(m):
            part[k, x] = direct[x * rows : (x + 1) * rows]
        for x in range(m):
            @pl.when((k != q) | (x != p))
            def _():
                part_copy(k, x).start()

    each(n, finish)

    total[pl.ds(0, rows), :] = part[q, p]

    def gather(i):
        z = lax.rem(q + lax.div(i, m), n)
        x = lax.rem(p + lax.rem(i, m), m)
        box = inbox.at[z, x]
        remote(box, box, part_send.at[z, x], part_recv.at[z, x], z, x).wait_recv()
        total[pl.ds(0, rows), :] += inbox[z, x]

    lax.fori_loop(1, n * m, lambda i, _: (gather(i), 0)[1], 0)

    out_rows = out_ref.shape[0]
    even = total[pl.ds(0, out_rows, stride=2), :]
    odd = total[pl.ds(1, out_rows, stride=2), :]
    summed = jnp.concatenate([even, odd], axis=1)
    own_amp = amp_all[q, pl.ds(p * out_rows, out_rows), :]
    gap = gaps[...]
    out_ref[...] = (gap * own_amp - summed) / (gap + shift_ref[0])

    def sent_small(d):
        z = lax.rem(q + d + 1, n)
        amp_copy(z).wait_send()
        val_copy(z).wait_send()

    each(n - 1, sent_small)

    def sent_con(s, _):
        for c in range(ch):
            block = con_all.at[s, p, c]

            @pl.when((q > 0) & (s >= q))
            def _():
                con_z(s, c, 0, block).wait_send()

            @pl.when((q < n - 1) & (s <= q))
            def _():
                con_z(s, c, 1, block).wait_send()

            for dx in range(1, m):
                con_x(s, c, dx, block).wait_send()
        return 0

    lax.fori_loop(0, n, sent_con, 0)

    def sent_part(i):
        z = lax.rem(q + lax.div(i, m), n)
        x = lax.rem(p + lax.rem(i, m), m)
        part_copy(z, x).wait_send()

    lax.fori_loop(1, n * m, lambda i, _: (sent_part(i), 0)[1], 0)


def shards(
    n, m,
    amplitudes, valence_orbitals, conduction_orbitals, screened, band_gaps, shifts, difference_table,
):
    nv, slab = valence_orbitals.shape[2:]
    nc = conduction_orbitals.shape[2]
    ch = 2 if n * m <= 16 else 1
    w = slab // ch
    points = screened.shape[2]
    amp_rows = amplitudes.shape[2] // LANES
    out_rows = band_gaps.shape[2] // LANES
    dma = pltpu.SemaphoreType.DMA
    flat = pl.pallas_call(
        functools.partial(kernel, n, m, ch),
        out_shape=jax.ShapeDtypeStruct((out_rows, LANES), F32),
        in_specs=[pl.BlockSpec(memory_space=pl.ANY)] * 5
        + [pl.BlockSpec(memory_space=pltpu.SMEM)] * 2,
        out_specs=pl.BlockSpec(memory_space=pltpu.VMEM),
        scratch_shapes=[
            pltpu.VMEM((n, amp_rows, LANES), F32),
            pltpu.VMEM((n, nv, slab), F32),
            pltpu.VMEM((n, m, ch, nc, w), F32),
            pltpu.VMEM((slab, points), F32),
            pltpu.VMEM((out_rows, LANES), F32),
            pltpu.VMEM((nv + 8, LANES), F32),
            pltpu.VMEM((n, 2 * nv, slab), BF16),
            pltpu.VMEM((n, m, ch, 4 * nc, w), BF16),
            pltpu.VMEM((n, slab, 4 * nc), BF16),
            pltpu.VMEM((n, m, ch, 2 * nv, w), BF16),
            pltpu.VMEM((n, m, nv // m, nc), F32),
            pltpu.VMEM((n, m, nv // m, nc), F32),
            pltpu.VMEM((nv // m + 8, nc), F32),
            dma((4 + ch,)),
            dma((n,)),
            dma((n,)),
            dma((n,)),
            dma((n,)),
            dma((n, m, ch)),
            dma((n, ch, 2)),
            dma((n, max(m - 1, 1), ch)),
            dma((n, m)),
            dma((n, m)),
        ],
        compiler_params=pltpu.CompilerParams(
            collective_id=0, has_side_effects=True, vmem_limit_bytes=56 * 1024 * 1024
        ),
        cost_estimate=pl.CostEstimate(
            flops=2 * n * slab * points * (nc + nv), bytes_accessed=4 * slab * points,
            transcendentals=0,
        ),
    )(
        amplitudes.reshape(amp_rows, LANES),
        valence_orbitals.reshape(nv, slab),
        conduction_orbitals.reshape(nc, slab),
        screened.reshape(slab, points),
        band_gaps.reshape(out_rows, LANES),
        shifts,
        difference_table,
    )
    return flat.reshape(band_gaps.shape)


def solution(mesh):
    placed = (
        P(("groups", "spin"), "pb", None),
        P(("groups", "spin"), "pb", None, "pt"),
        P(("groups", "spin"), "pb", None, "pt"),
        P(("groups", "pb"), "pt", None),
        P(("groups", "spin"), "pb", "pt"),
        P(("groups", "spin")),
        P(),
    )
    return jax.shard_map(
        functools.partial(shards, mesh.shape["pb"], mesh.shape["pt"]),
        mesh=mesh,
        in_specs=placed,
        out_specs=P(("groups", "spin"), "pb", "pt"),
        check_vma=False,
    )
```

time: 116 us -> 36.4 us (0.31)
  blocking collectives: 57.5 us -> 0 us
  Pallas kernels: 0 us -> 34.3 us
  waiting for transfers between devices: 17.4 us -> 0 us
  matrix products: 13.8 us -> 0 us
  between operations: 14.2 us -> 0.66 us
  local copies, waits for them, and re-layouts: 10.6 us -> 1.28 us
  other arithmetic: 2.42 us -> 0 us
    all_gather x3 -> x0, blocking collectives: 38.9 us -> none  [the longest x1 16.3 us: shards(): lax.all_gather(valence_orbitals, 'pb', axis=1, tiled=True)]
    pallas_call x0 -> x1, Pallas kernels: none -> 34.3 us  [shards(): pl.pallas_call(functools.partial(kernel, n, m, ch), out_shape=jax.ShapeDt...]
    unnamed x1 -> x0, blocking collectives: 18.5 us -> none
    unnamed x3 -> x0, waiting for transfers between devices: 17.4 us -> none
    dot_general x4 -> x0, matrix products: 13.8 us -> none  [the longest x1 6.89 us: pair_block(): jnp.einsum('bcm,bpcs->bmps', mixed, source_con, precision=lax.Precision.H...]
    gather x6 -> x0, local copies, waits for them, and re-layouts: 5.48 us -> none  [the longest x2 3.68 us: fetch_rows(): return jnp.take(conduction_rows, ids, axis=0)[:, None]]
    unnamed x11 -> x1, local copies, waits for them, and re-layouts: 5 us -> 1.28 us
  transfers between devices with their start and end apart: 2 -> 0, of which waited for: 1 -> 0; matrix products, arithmetic and copies ran while one was open for 5% -> 0% of each run, Pallas kernels for 0% -> 0%
where the time goes in v1:
time: 36.4 us; the launch traced here: 36.2 us
  Pallas kernels  34.3 us (94%)
  local copies, waits for them, and re-layouts  1.28 us (4%)
  between operations  0.66 us (2%)
    pallas_call x1, Pallas kernels, shards(): pl.pallas_call(functools.partial(kernel, n, m, ch), out_shape=jax.ShapeDt...  34.3 us
    unnamed x1, local copies, waits for them, and re-layouts  1.28 us

profile of v1, /device:TPU:0, one launch (start us, length us, event | category | flops | bytes accessed | tf_op | source)
XLA Modules:
  0.0 36.2 jit_solution(7242813613689624031)
XLA Ops:
  0.7 34.3 %shard_map.73 = f32[8,128]{1,0:T(8,128)} custom-call(f32[16,128]{1,0:T(8,128)} %bitcast.10, f32[32,512]{1,0:T(8,128)} %bitcast.8, f32[64,512]{1,0:T(8,128)} %bitcast.7, f32[512,1024]{1,0:T(8,128)} %bitcast.6, f32[8,128]{1,0:T(8,128)} %bitcast.11, f32[1]{0:T(128)S(6)} %copy.9.shift_ref, s32[4,4]{1,0:T(4,128)} %table_ref.1), custom_call_target="tpu_custom_call" | custom-call | flops 402653184 | bytes 2097152 | tf_op jit(solution)/shard_map/pallas_call | solution.py:341
  35.0 1.3 %copy.10 = f32[1,1,1024]{2,1,0:T(1,128)} copy(f32[1,1,1024]{2,1,0:T(1,128)} %bitcast.9) | data formatting | bytes 8192

commit v2 on v1

--- a/solution.py
+++ b/solution.py
@@ -30,13 +30,13 @@
 
 
 def kernel(
-    n, m, ch,
+    n, m, ch, pieces,
     amp_ref, val_ref, con_ref, scr_ref, gap_ref, shift_ref, table_ref,
     out_ref,
     amp_all, val_all, con_all, weight, gaps,
     amp_wide, val_stack, con_stack, mix, half_stack, part, inbox, total,
-    load_sem, amp_send, amp_recv, val_send, val_recv, con_recv,
-    conz_send, conx_send, part_send, part_recv,
+    load_sem, amp_send, amp_recv, val_send, val_recv,
+    con_send, conx_send, con_recv, part_send, part_recv,
 ):
     nv, slab = val_ref.shape
     nc = con_ref.shape[0]
@@ -67,63 +67,75 @@
         pltpu.make_async_copy(val_ref, val_all.at[q], load_sem.at[1]),
         pltpu.make_async_copy(gap_ref, gaps, load_sem.at[2]),
         pltpu.make_async_copy(scr_ref, weight, load_sem.at[3]),
-    ] + [
-        pltpu.make_async_copy(
-            con_ref.at[:, pl.ds(c * w, w)], con_all.at[q, p, c], load_sem.at[4 + c]
-        )
-        for c in range(ch)
+        pltpu.make_async_copy(con_ref, con_all.at[q, p], load_sem.at[4]),
     ]
     for load in loads:
         load.start()
 
     pl.semaphore_wait(barrier, n * m - 1)
 
-    def val_copy(z):
-        return remote(val_ref, val_all.at[q], val_send.at[z], val_recv.at[q], z, p)
-
-    def amp_copy(z):
-        return remote(amp_ref, amp_all.at[q], amp_send.at[z], amp_recv.at[q], z, p)
+    def small_copies(z):
+        return (
+            remote(val_ref, val_all.at[q], val_send.at[z], val_recv.at[q], z, p),
+            remote(amp_ref, amp_all.at[q], amp_send.at[z], amp_recv.at[q], z, p),
+        )
+
+    def small_wait(s):
+        for ref, send, recv in ((val_all, val_send, val_recv), (amp_all, amp_send, amp_recv)):
+            remote(ref.at[s], ref.at[s], send.at[s], recv.at[s], s, p).wait_recv()
+
+    def rows_of(r):
+        return pl.ds(r * (nc // pieces), nc // pieces)
+
+    def con_z(s, r, side, src):
+        z = q - 1 if side == 0 else q + 1
+        spot = con_all.at[s, p, rows_of(r)]
+        return remote(src, spot, con_send.at[s, r, side], con_recv.at[s, p, r], z, p)
+
+    def con_x(s, r, dx, src):
+        spot = con_all.at[s, p, rows_of(r)]
+        return remote(
+            src, spot, conx_send.at[s, dx - 1, r], con_recv.at[s, p, r], q, lax.rem(p + dx, m)
+        )
+
+    def con_wait(s, x, r):
+        spot = con_all.at[s, x, rows_of(r)]
+        remote(
+            spot, spot, con_send.at[s, r, 0], con_recv.at[s, x, r], q, lax.rem(p + 1, m)
+        ).wait_recv()
+
+    def toward(side):
+        return (q > 0) if side == 0 else (q < n - 1)
+
+    def both(t, act):
+        pl.when(q + t < n)(lambda: act(q + t, 0))
+        pl.when(q - t >= 0)(lambda: act(q - t, 1))
+
+    def forward(t):
+        for r in range(pieces):
+            def take(s, side):
+                con_wait(s, p, r)
+                block = con_all.at[s, p, rows_of(r)]
+                pl.when(toward(side))(lambda: con_z(s, r, side, block).start())
+                for dx in range(1, m):
+                    con_x(s, r, dx, block).start()
+
+            both(t, take)
 
     def send_small(d):
-        z = lax.rem(q + d + 1, n)
-        amp_copy(z).start()
-        val_copy(z).start()
-
+        for copy in small_copies(lax.rem(q + d + 1, n)):
+            copy.start()
+
+    for r in range(pieces):
+        for side in range(2):
+            pl.when(toward(side))(lambda: con_z(q, r, side, con_ref.at[rows_of(r)]).start())
+        for dx in range(1, m):
+            con_x(q, r, dx, con_ref.at[rows_of(r)]).start()
     each(n - 1, send_small)
-
-    def con_z(s, c, side, src):
-        z = q - 1 if side == 0 else q + 1
-        return remote(
-            src, con_all.at[s, p, c], conz_send.at[s, c, side], con_recv.at[s, p, c], z, p
-        )
-
-    def con_x(s, c, dx, src):
-        x = lax.rem(p + dx, m)
-        return remote(
-            src, con_all.at[s, p, c], conx_send.at[s, dx - 1, c], con_recv.at[s, p, c], q, x
-        )
-
-    def con_wait(s, x, c):
-        block = con_all.at[s, x, c]
-        pltpu.make_async_remote_copy(
-            src_ref=block, dst_ref=block, send_sem=conz_send.at[s, c, 0],
-            recv_sem=con_recv.at[s, x, c], device_id=at(q, lax.rem(p + 1, m)),
-            device_id_type=pl.DeviceIdType.MESH,
-        ).wait_recv()
-
-    for c in range(ch):
-        own = con_ref.at[:, pl.ds(c * w, w)]
-
-        @pl.when(q > 0)
-        def _():
-            con_z(q, c, 0, own).start()
-
-        @pl.when(q < n - 1)
-        def _():
-            con_z(q, c, 1, own).start()
-
-        for dx in range(1, m):
-            con_x(q, c, dx, own).start()
+    if n > 1:
+        forward(1)
+    if n > 2:
+        forward(2)
 
     def prepare(s):
         rows = amp_all[s]
@@ -156,15 +168,16 @@
         )
 
     def unit(s, x, c, target):
-        c_hi, c_lo = split(con_all[s, x, c])
+        lanes = pl.ds(pl.multiple_of(c * w, w), w)
+        c_hi, c_lo = split(con_all[s, x, :, lanes])
         stack = jnp.concatenate([c_hi, c_hi, c_lo, c_lo], axis=0)
         con_stack[s, x, c] = stack
         columns = pl.ds(pl.multiple_of(x * slab + c * w, w), w)
         pairs = dot(mix[s], stack) * weight[:, columns]
         p_hi, p_lo = split(pairs)
         bands = val_stack[target]
-        both = dot(bands, p_hi) + dot(bands, p_lo)
-        half = both[:nv] + both[nv:]
+        products = dot(bands, p_hi) + dot(bands, p_lo)
+        half = products[:nv] + products[nv:]
         h_hi, h_lo = split(half)
         half_stack[s, x, c] = jnp.concatenate([h_hi, h_lo], axis=0)
 
@@ -173,16 +186,14 @@
         lax.fori_loop(0, ch, lambda c, _: (unit(s, x, c, target), 0)[1], 0)
 
     def crossed(s):
-        target = target_of(s)
-
         def step(i, _):
-            x = lax.rem(p + 1 + lax.div(i, ch), m)
-            c = lax.rem(i, ch)
-            con_wait(s, x, c)
-            unit(s, x, c, target)
+            x = lax.rem(p + 1 + i, m)
+            for r in range(pieces):
+                con_wait(s, x, r)
+            units(s, x)
             return 0
 
-        lax.fori_loop(0, (m - 1) * ch, step, 0)
+        lax.fori_loop(0, m - 1, step, 0)
 
     for load in loads:
         load.wait()
@@ -190,62 +201,24 @@
 
     def take_small(d):
         s = lax.rem(q + d + 1, n)
-        remote(amp_all.at[s], amp_all.at[s], amp_send.at[s], amp_recv.at[s], s, p).wait_recv()
-        remote(val_all.at[s], val_all.at[s], val_send.at[s], val_recv.at[s], s, p).wait_recv()
+        small_wait(s)
         prepare(s)
 
     lax.fori_loop(0, n - 1, lambda d, _: (take_small(d), 0)[1], 0)
 
     units(q, p)
-
-    def forward(s, side):
-        for c in range(ch):
-            con_wait(s, p, c)
-            block = con_all.at[s, p, c]
-
-            @pl.when((q > 0) if side == 0 else (q < n - 1))
-            def _():
-                con_z(s, c, side, block).start()
-
-            for dx in range(1, m):
-                con_x(s, c, dx, block).start()
+    crossed(q)
 
     def walk(t, _):
-        @pl.when(q + t < n)
-        def _():
-            forward(q + t, 0)
-
-        @pl.when(q - t >= 0)
-        def _():
-            forward(q - t, 1)
-
-        @pl.when(q + t < n)
-        def _():
-            units(q + t, p)
-
-        @pl.when(q - t >= 0)
-        def _():
-            units(q - t, p)
-
-        @pl.when(q + t - 1 < n)
-        def _():
-            crossed(q + t - 1)
-
-        @pl.when((q - t + 1 >= 0) & (t > 1))
-        def _():
-            crossed(q - t + 1)
-
+        both(t - 1, lambda s, side: units(s, p))
+        pl.when(t > 2)(lambda: forward(t))
+        both(t - 1, lambda s, side: crossed(s))
         return 0
 
-    lax.fori_loop(1, n, walk, 0)
-
-    @pl.when(q + n - 1 < n)
-    def _():
-        crossed(q + n - 1)
-
-    @pl.when((q - n + 1 >= 0) & (n > 1))
-    def _():
-        crossed(q - n + 1)
+    lax.fori_loop(2, n, walk, 0)
+    if n > 1:
+        both(n - 1, lambda s, side: units(s, p))
+        both(n - 1, lambda s, side: crossed(s))
 
     def part_copy(k, x):
         return remote(
@@ -274,16 +247,20 @@
 
     each(n, finish)
 
-    total[pl.ds(0, rows), :] = part[q, p]
-
-    def gather(i):
+    def gather(i, summed):
         z = lax.rem(q + lax.div(i, m), n)
         x = lax.rem(p + lax.rem(i, m), m)
         box = inbox.at[z, x]
         remote(box, box, part_send.at[z, x], part_recv.at[z, x], z, x).wait_recv()
-        total[pl.ds(0, rows), :] += inbox[z, x]
-
-    lax.fori_loop(1, n * m, lambda i, _: (gather(i), 0)[1], 0)
+        return summed + inbox[z, x]
+
+    summed = part[q, p]
+    if n * m <= 16:
+        for i in range(1, n * m):
+            summed = gather(i, summed)
+    else:
+        summed = lax.fori_loop(1, n * m, gather, summed)
+    total[pl.ds(0, rows), :] = summed
 
     out_rows = out_ref.shape[0]
     even = total[pl.ds(0, out_rows, stride=2), :]
@@ -294,26 +271,18 @@
     out_ref[...] = (gap * own_amp - summed) / (gap + shift_ref[0])
 
     def sent_small(d):
-        z = lax.rem(q + d + 1, n)
-        amp_copy(z).wait_send()
-        val_copy(z).wait_send()
+        for copy in small_copies(lax.rem(q + d + 1, n)):
+            copy.wait_send()
 
     each(n - 1, sent_small)
 
     def sent_con(s, _):
-        for c in range(ch):
-            block = con_all.at[s, p, c]
-
-            @pl.when((q > 0) & (s >= q))
-            def _():
-                con_z(s, c, 0, block).wait_send()
-
-            @pl.when((q < n - 1) & (s <= q))
-            def _():
-                con_z(s, c, 1, block).wait_send()
-
+        for r in range(pieces):
+            block = con_all.at[s, p, rows_of(r)]
+            pl.when(toward(0) & (s >= q))(lambda: con_z(s, r, 0, block).wait_send())
+            pl.when(toward(1) & (s <= q))(lambda: con_z(s, r, 1, block).wait_send())
             for dx in range(1, m):
-                con_x(s, c, dx, block).wait_send()
+                con_x(s, r, dx, block).wait_send()
         return 0
 
     lax.fori_loop(0, n, sent_con, 0)
@@ -332,14 +301,15 @@
 ):
     nv, slab = valence_orbitals.shape[2:]
     nc = conduction_orbitals.shape[2]
-    ch = 2 if n * m <= 16 else 1
+    ch = 1
+    pieces = 2 if n * m <= 16 else 1
     w = slab // ch
     points = screened.shape[2]
     amp_rows = amplitudes.shape[2] // LANES
     out_rows = band_gaps.shape[2] // LANES
     dma = pltpu.SemaphoreType.DMA
     flat = pl.pallas_call(
-        functools.partial(kernel, n, m, ch),
+        functools.partial(kernel, n, m, ch, pieces),
         out_shape=jax.ShapeDtypeStruct((out_rows, LANES), F32),
         in_specs=[pl.BlockSpec(memory_space=pl.ANY)] * 5
         + [pl.BlockSpec(memory_space=pltpu.SMEM)] * 2,
@@ -347,7 +317,7 @@
         scratch_shapes=[
             pltpu.VMEM((n, amp_rows, LANES), F32),
             pltpu.VMEM((n, nv, slab), F32),
-            pltpu.VMEM((n, m, ch, nc, w), F32),
+            pltpu.VMEM((n, m, nc, slab), F32),
             pltpu.VMEM((slab, points), F32),
             pltpu.VMEM((out_rows, LANES), F32),
             pltpu.VMEM((nv + 8, LANES), F32),
@@ -358,14 +328,14 @@
             pltpu.VMEM((n, m, nv // m, nc), F32),
             pltpu.VMEM((n, m, nv // m, nc), F32),
             pltpu.VMEM((nv // m + 8, nc), F32),
-            dma((4 + ch,)),
+            dma((5,)),
             dma((n,)),
             dma((n,)),
             dma((n,)),
             dma((n,)),
-            dma((n, m, ch)),
-            dma((n, ch, 2)),
-            dma((n, max(m - 1, 1), ch)),
+            dma((n, pieces, 2)),
+            dma((n, max(m - 1, 1), pieces)),
+            dma((n, m, pieces)),
             dma((n, m)),
             dma((n, m)),
         ],

time: 36.4 us -> 34.9 us (0.959)
  Pallas kernels: 34.3 us -> 32.8 us
    pallas_call x1, Pallas kernels: 34.3 us -> 32.8 us  [shards(): pl.pallas_call(functools.partial(kernel, n, m, ch, pieces), out_shape=jax...]
where the time goes in v2:
time: 34.9 us; the launch traced here: 34.7 us
  Pallas kernels  32.8 us (94%)
  local copies, waits for them, and re-layouts  1.28 us (4%)
  between operations  0.66 us (2%)
    pallas_call x1, Pallas kernels, shards(): pl.pallas_call(functools.partial(kernel, n, m, ch, pieces), out_shape=jax...  32.8 us
    unnamed x1, local copies, waits for them, and re-layouts  1.28 us

profile of v2, /device:TPU:0, one launch (start us, length us, event | category | flops | bytes accessed | tf_op | source)
XLA Modules:
  0.0 34.7 jit_solution(661047705929055448)
XLA Ops:
  0.7 32.8 %shard_map.73 = f32[8,128]{1,0:T(8,128)} custom-call(f32[16,128]{1,0:T(8,128)} %bitcast.10, f32[32,512]{1,0:T(8,128)} %bitcast.8, f32[64,512]{1,0:T(8,128)} %bitcast.7, f32[512,1024]{1,0:T(8,128)} %bitcast.6, f32[8,128]{1,0:T(8,128)} %bitcast.11, f32[1]{0:T(128)S(6)} %copy.9.shift_ref, s32[4,4]{1,0:T(4,128)} %table_ref.1), custom_call_target="tpu_custom_call" | custom-call | flops 402653184 | bytes 2097152 | tf_op jit(solution)/shard_map/pallas_call | solution.py:311
  33.5 1.3 %copy.10 = f32[1,1,1024]{2,1,0:T(1,128)} copy(f32[1,1,1024]{2,1,0:T(1,128)} %bitcast.9) | data formatting | bytes 8192

commit v3 on v2

--- a/solution.py
+++ b/solution.py
@@ -123,7 +123,7 @@
             both(t, take)
 
     def send_small(d):
-        for copy in small_copies(lax.rem(q + d + 1, n)):
+        for copy in small_copies(lax.rem(q + lax.rem(d + n // 2, n - 1) + 1, n)):
             copy.start()
 
     for r in range(pieces):

time: 34.9 us -> 34.9 us (level)
  no operation moved by 1% of the time
where the time goes in v3:
time: 34.9 us; the launch traced here: 34.7 us
  Pallas kernels  32.8 us (94%)
  local copies, waits for them, and re-layouts  1.28 us (4%)
  between operations  0.66 us (2%)
    pallas_call x1, Pallas kernels, shards(): pl.pallas_call(functools.partial(kernel, n, m, ch, pieces), out_shape=jax...  32.8 us
    unnamed x1, local copies, waits for them, and re-layouts  1.28 us

profile of v3, /device:TPU:0, one launch (start us, length us, event | category | flops | bytes accessed | tf_op | source)
XLA Modules:
  0.0 34.7 jit_solution(1748441717870488347)
XLA Ops:
  0.7 32.8 %shard_map.73 = f32[8,128]{1,0:T(8,128)} custom-call(f32[16,128]{1,0:T(8,128)} %bitcast.10, f32[32,512]{1,0:T(8,128)} %bitcast.8, f32[64,512]{1,0:T(8,128)} %bitcast.7, f32[512,1024]{1,0:T(8,128)} %bitcast.6, f32[8,128]{1,0:T(8,128)} %bitcast.11, f32[1]{0:T(128)S(6)} %copy.9.shift_ref, s32[4,4]{1,0:T(4,128)} %table_ref.1), custom_call_target="tpu_custom_call" | custom-call | flops 402653184 | bytes 2097152 | tf_op jit(solution)/shard_map/pallas_call | solution.py:311
  33.5 1.3 %copy.10 = f32[1,1,1024]{2,1,0:T(1,128)} copy(f32[1,1,1024]{2,1,0:T(1,128)} %bitcast.9) | data formatting | bytes 8192
